TPU v7x, 32 devices: a whole 2x2x4 slice. The times are simulated.
32 devices in a mesh: row: 8 (over z, y), col: 4 (over x, core).
Axes of the slice: x: 2, y: 2, z: 4, core: 2. Of those that a mesh axis runs over, the one named last changes fastest.
Arguments:
- panel: bfloat16 [2, 8, 512, 4, 512], P(None, 'row', None, 'col'), may hold values from -0.25 to 0.25
- rhs: float32 [2, 8, 512, 2048], P(None, 'row', None, 'col'), may hold values from -6 to 6
- inverse: bfloat16 [4, 512, 512], replicated, as said below
Outputs:
- solved: float32 [4, 512, 2048], P(None, None, 'col')
- remainder: float32 [2, 8, 512, 2048], P(None, 'row', None, 'col')
Inputs may be any that keep to these rules, and one draw needn't show every extreme that they name: Each block of inverse is lower triangular with a positive diagonal.
All inputs are finite; a program needn't handle non-finite values.
Results may differ from a plain program's by a relative error of at most 0.008.
Values may be sent and summed in bfloat16 or wider, within the bound.
A program may use at most 128 MiB of HBM per device.

v0:
```python
import jax
import jax.numpy as jnp
from jax import lax
from jax.sharding import PartitionSpec as P


def from_root(x, axis, root):
    mine = lax.axis_index(axis) == root
    return lax.psum(jnp.where(mine, x, jnp.zeros_like(x)), axis)


def on_device(panel, rhs, inverse):
    steps = inverse.shape[0]
    block = panel.shape[2]
    local_cols = rhs.shape[3]
    row_count = panel.shape[0]
    n_rows = lax.axis_size("row")
    offset = n_rows - steps
    row_index = lax.axis_index("row")
    first_row = panel[0, 0, :, 0, :]
    row_blocks = lax.all_gather(first_row, "col", axis=1, tiled=True)
    own_rhs = rhs[0, 0]
    solved = jnp.zeros((steps, block, local_cols), jnp.float32)
    for step in range(steps):
        base = own_rhs
        if step > 0:
            lower = solved[:step].astype(jnp.bfloat16).reshape(step * block, local_cols)
            base = base - jnp.dot(
                row_blocks[:, : step * block], lower, preferred_element_type=jnp.float32
            )
        fresh = jnp.dot(
            inverse[step], base.astype(jnp.bfloat16), preferred_element_type=jnp.float32
        )
        fresh = from_root(fresh, "row", offset + step)
        solved = solved.at[step].set(fresh)
    low_solved = solved.astype(jnp.bfloat16)
    block_rows = jnp.arange(row_count, dtype=jnp.int32) * n_rows + row_index
    piece = lax.all_gather(panel, "col", axis=3, tiled=True)
    count = piece.shape[3]
    columns = jnp.arange(count, dtype=jnp.int32)
    keep = (columns[None, :] + offset < block_rows[:, None]).astype(jnp.bfloat16)
    masked = piece[:, 0] * keep[:, None, :, None]
    update = jnp.einsum("qajb,jbn->qan", masked, low_solved, preferred_element_type=jnp.float32)
    remainder = (rhs[:, 0] - update)[:, None]
    return (solved, remainder)


def solution(mesh):
    placed = (P(None, "row", None, "col", None), P(None, "row", None, "col"), P())
    return jax.shard_map(
        on_device,
        mesh=mesh,
        in_specs=placed,
        out_specs=(P(None, None, "col"), P(None, "row", None, "col")),
        check_vma=False,
    )
```

profile of v0, /device:TPU:2, one launch (start us, length us, event | category | flops | bytes accessed | tf_op | source)
XLA Modules:
  0.0 363.5 jit_solution(8520836090424650376)
XLA Ops:
  8.0 0.0 copy-start.1
  8.0 0.0 all-reduce.6.cloned.1.call-start
  8.1 0.0 copy-start.2
  8.1 2.9 convolution_select_fusion.3
  11.0 0.0 all-reduce.6.cloned.1.call-update
  11.0 0.0 all-gather.6.cloned.1.call-start
  11.1 0.0 copy-done.1
  11.1 0.8 slice.120
  11.9 0.0 all-gather.6.cloned.1.call-update
  12.0 0.0 all-reduce.8.cloned.1.call-start
  12.0 80.2 %all-reduce.6.cloned.1.call-done = f32[512,512]{1,0:T(8,128)} async-done(((f32[512,512]{1,0:T(8,128)}), f32[512,512]{1,0:T(8,128)}) %all-reduce.6.cloned.1.call-update) | async-done | bytes 1048592 | tf_op jit(solution)/shard_map/psum | solution.py:9
  92.2 0.0 all-gather.6.cloned.1.call-done
  92.2 0.0 copy-done.2
  92.2 0.0 copy-start
  92.2 3.4 fusion.11
  95.6 0.0 all-reduce.8.cloned.1.call-update
  95.6 0.0 all-reduce.10.cloned.1.call-start
  95.6 0.0 copy-done
  95.7 2.6 scatter.14
  98.2 76.0 %all-reduce.8.cloned.1.call-done = f32[1,512,512]{2,1,0:T(8,128)} async-done(((f32[1,512,512]{2,1,0:T(8,128)}), f32[1,512,512]{2,1,0:T(8,128)}) %all-reduce.8.cloned.1.call-update) | async-done | bytes 1048592 | tf_op jit(solution)/shard_map/psum | solution.py:9
  174.3 2.3 constant_dynamic-update-slice_fusion.2
  176.5 1.7 slice.184
  178.3 3.4 fusion.10
  181.7 0.0 all-reduce.10.cloned.1.call-update
  181.7 0.0 all-reduce.12.cloned.1.call-start
  181.8 77.7 %all-reduce.10.cloned.1.call-done = f32[1,512,512]{2,1,0:T(8,128)} async-done(((f32[1,512,512]{2,1,0:T(8,128)}), f32[1,512,512]{2,1,0:T(8,128)}) %all-reduce.10.cloned.1.call-update) | async-done | bytes 1048592 | tf_op jit(solution)/shard_map/psum | solution.py:9
  259.4 2.3 constant_dynamic-update-slice_fusion.1
  261.7 3.2 slice.183
  264.9 4.3 %fusion.9 = f32[1,512,512]{2,1,0:T(8,128)} fusion(bf16[1536,512]{1,0:T(8,128)(2,1)} %bitcast.89, bf16[512,2048]{1,0:T(8,128)(2,1)} %bitcast.93, f32[2,1,512,512]{3,2,1,0:T(8,128)S(1)} %copy-done.2, bf16[4,512,512]{2,1,0:T(8,128)(2,1)} %param.13, pred[]{:T(512)S(6)} %eq.15), kind=kOutput, calls=%fused_computation.12 | convolution fusion | flops 1074528256 | bytes 5767169 | tf_op jit(solution)/shard_map/dot_general | solution.py:31
  269.2 0.0 all-reduce.12.cloned.1.call-update
  269.3 0.0 all-gather.4.cloned.1.call-start
  269.3 0.5 all-gather.4.cloned.1.call-update
  269.9 0.1 compare_convert_fusion
  269.9 77.1 %all-reduce.12.cloned.1.call-done = f32[1,512,512]{2,1,0:T(8,128)} async-done(((f32[1,512,512]{2,1,0:T(8,128)}), f32[1,512,512]{2,1,0:T(8,128)}) %all-reduce.12.cloned.1.call-update) | async-done | bytes 1048592 | tf_op jit(solution)/shard_map/psum | solution.py:9
  347.0 2.3 constant_dynamic-update-slice_fusion
  349.3 0.0 all-gather.4.cloned.1.call-done
  349.3 7.1 %fusion.1 = f32[2,1,512,512]{3,2,1,0:T(8,128)} fusion(f32[2,1,512,512]{3,2,1,0:T(8,128)S(1)} %copy-done.2, f32[4,512,512]{2,1,0:T(8,128)} %constant_dynamic-update-slice_fusion, bf16[2,1,512,4,512]{4,2,3,1,0:T(8,128)(2,1)} %all-gather.4.cloned.1.call-done, bf16[2,4]{1,0:T(2,128)(2,1)S(1)} %compare_convert_fusion), kind=kOutput, calls=%fused_computation.5 | convolution fusion | flops 2151153664 | bytes 12582928 | tf_op jit(solution)/shard_map/qajb,jbn->qan/dot_general | solution.py:43
  (2 shorter events, 0.0 us)
Async XLA Ops:
  8.0 3.1 copy-start.1
  8.0 84.2 %all-reduce.6.cloned.1.call-start = ((), (), s32[]{:S(2)}) async-start(), calls=%async_computation | async-start | bytes 2097152 | tf_op jit(solution)/shard_map/psum | solution.py:9
  8.1 84.1 %copy-start.2 = (f32[2,1,512,512]{3,2,1,0:T(8,128)S(1)}, f32[2,1,512,512]{3,2,1,0:T(8,128)}, u32[]{:S(2)}) copy-start(f32[2,1,512,512]{3,2,1,0:T(8,128)} %param.12) | copy-start | bytes 6291460
  11.0 81.1 %all-gather.6.cloned.1.call-start = ((), (), s32[]{:S(2)}) async-start(), calls=%async_computation.5 | async-start | bytes 2621440 | tf_op jit(solution)/shard_map/all_gather | solution.py:21
  12.0 162.3 %all-reduce.8.cloned.1.call-start = ((), (), s32[]{:S(2)}) async-start(), calls=%async_computation.1 | async-start | bytes 2097152 | tf_op jit(solution)/shard_map/psum | solution.py:9
  92.2 3.5 copy-start
  95.6 163.8 %all-reduce.10.cloned.1.call-start = ((), (), s32[]{:S(2)}) async-start(), calls=%async_computation.2 | async-start | bytes 2097152 | tf_op jit(solution)/shard_map/psum | solution.py:9
  181.7 165.3 %all-reduce.12.cloned.1.call-start = ((), (), s32[]{:S(2)}) async-start(), calls=%async_computation.3 | async-start | bytes 2097152 | tf_op jit(solution)/shard_map/psum | solution.py:9
  269.3 80.0 %all-gather.4.cloned.1.call-start = ((), (), s32[]{:S(2)}) async-start(), calls=%async_computation.4 | async-start | bytes 5242880 | tf_op jit(solution)/shard_map/all_gather | solution.py:38
Sparse Core Ops, SparseCore 0:
  12.9 79.2 all-reduce.5
  96.7 77.5 all-reduce.7
  181.8 77.5 all-reduce.9
  269.4 77.5 all-reduce.11
Sparse Core Ops, SparseCore 1:
  13.7 22.5 all-gather.5
  271.3 32.8 all-gather.3
where the time goes:
time: 365 us; the launch traced here: 364 us
  waiting for transfers between devices  312 us (85%)
  matrix products  21.2 us (6%)
  between operations  15.3 us (4%)
  local copies, waits for them, and re-layouts  15.2 us (4%)
    psum x4, waiting for transfers between devices, from_root(): return lax.psum(jnp.where(mine, x, jnp.zeros_like(x)), axis)  311 us
    dot_general x4, matrix products, on_device(): jnp.dot(inverse[step], base.astype(jnp.bfloat16), preferred_element_type=...  14.1 us
    scatter x4, local copies, waits for them, and re-layouts, on_device(): solved = solved.at[step].set(fresh)  9.36 us
  transfers between devices with their start and end apart: 6, of which 4 were waited for; matrix products, arithmetic and copies ran while one was open for 2% of the time, Pallas kernels for 0%

commit v1 on v0

v1 whole, which is shorter than its diff:
```python
import functools

import jax
import jax.numpy as jnp
from jax import lax
from jax.experimental import pallas as pl
from jax.experimental.pallas import tpu as pltpu
from jax.sharding import PartitionSpec as P

MESH = pl.DeviceIdType.MESH


def kernel(
    n_rows, n_cols, steps, panel, rhs, inverse, low_out, rem_out,
    low, acc, inv, lower,
    load_sem, own_sem, inv_sem, low_sem, rem_sem, send_sem, recv_sem, psend_sem, precv_sem,
):
    rb = acc.shape[0]
    chunks, width = acc.shape[1], acc.shape[3]
    offset = n_rows - steps
    levels = n_rows // 2
    bits = [1 << b for b in reversed(range(n_cols.bit_length() - 1))]
    row, col = lax.axis_index("row"), lax.axis_index("col")
    level, side = row // 2, row % 2
    mine = row - offset
    inv_index = jnp.maximum(mine, 0)

    def flip(bit):
        return col + bit - 2 * bit * ((col // bit) % 2)

    targets = (row + 1 - 2 * side, row - 2, row + 2)
    exists = (level >= 0, level > 0, level < levels - 1)

    def columns(t):
        return pl.ds(pl.multiple_of(t * width, width), width)

    def load(q, t):
        return pltpu.make_async_copy(rhs.at[q, :, columns(t)], acc.at[q, t], load_sem.at[q, t])

    def load_own(q):
        return pltpu.make_async_copy(panel.at[q], lower.at[q, col], own_sem.at[q])

    load_inv = pltpu.make_async_copy(inverse.at[inv_index], inv, inv_sem)

    def store_low(k, t):
        return pltpu.make_async_copy(low.at[k, t], low_out.at[k, :, columns(t)], low_sem.at[k, t])

    def store_rem(q, t):
        return pltpu.make_async_copy(acc.at[q, t], rem_out.at[q, :, columns(t)], rem_sem.at[q, t])

    def send_low(way, k, t):
        return pltpu.make_async_remote_copy(
            src_ref=low.at[k, t], dst_ref=low.at[k, t],
            send_sem=send_sem.at[way, k, t], recv_sem=recv_sem.at[k, t],
            device_id={"row": targets[way]}, device_id_type=MESH,
        )

    def goes(way, k):
        home = (offset + k) // 2
        same = k % 2 == side
        if way == 0:
            return same
        if way == 1:
            return same & (level > 0) & (level <= home)
        return same & (level < levels - 1) & (level >= home)

    def forward(k, t):
        for way in range(3):
            @pl.when(goes(way, k))
            def _():
                send_low(way, k, t).start()

    def send_block(q, j, b):
        return pltpu.make_async_remote_copy(
            src_ref=lower.at[q, j], dst_ref=lower.at[q, j],
            send_sem=psend_sem.at[q, j, b], recv_sem=precv_sem.at[q, j],
            device_id={"col": flip(bits[b])}, device_id_type=MESH,
        )

    def send_own(q):
        load_own(q).wait()
        for b in range(len(bits)):
            send_block(q, col, b).start()

    def passes(j, b):
        return (col % (2 * bits[b])) == (j % (2 * bits[b]))

    def receive_block(q, j):
        @pl.when(col != j)
        def _():
            send_block(q, j, 0).wait_recv()
            for b in range(len(bits)):
                @pl.when(passes(j, b))
                def _():
                    send_block(q, j, b).start()

    @pl.when(mine >= 0)
    def _():
        load_inv.start()

    @pl.loop(0, chunks)
    def _(t):
        load(0, t).start()

    for q in range(rb):
        load_own(q).start()
    for q in range(1, rb):
        @pl.loop(0, chunks)
        def _(t):
            load(q, t).start()

    barrier = pltpu.get_barrier_semaphore()
    for way in range(3):
        @pl.when(exists[way])
        def _():
            pl.semaphore_signal(barrier, inc=1, device_id={"row": targets[way]}, device_id_type=MESH)
    for bit in bits:
        pl.semaphore_signal(barrier, inc=1, device_id={"col": flip(bit)}, device_id_type=MESH)
    pl.semaphore_wait(
        barrier,
        1 + len(bits) + jnp.minimum(level, 1) + jnp.minimum(levels - 1 - level, 1),
    )

    @pl.when(mine > col)
    def _():
        send_own(0)

    @pl.when(mine <= col)
    def _():
        load_own(0).wait()

    def send_later():
        for q in range(1, rb):
            send_own(q)

    @pl.when(mine < 1)
    def _():
        send_later()

    @pl.loop(0, chunks)
    def _(t):
        load(0, t).wait()

    def produce(t):
        @pl.loop(0, inv_index)
        def _(j):
            acc[0, t] -= jnp.dot(lower[0, j], low[j, t], preferred_element_type=jnp.float32)

        low[inv_index, t] = jnp.dot(
            inv[...], acc[0, t].astype(jnp.bfloat16), preferred_element_type=jnp.float32
        ).astype(jnp.bfloat16)
        forward(inv_index, t)
        store_low(inv_index, t).start()
        store_rem(0, t).start()

    @pl.when(mine >= 0)
    def _():
        load_inv.wait()

    @pl.when(mine == 0)
    def _():
        @pl.loop(0, chunks)
        def _(t):
            produce(t)

    @pl.when(mine < 0)
    def _():
        @pl.loop(0, chunks)
        def _(t):
            store_rem(0, t).start()

    gather_at = (steps - 1 - side) * chunks
    last = steps - 1 - side

    @pl.loop(0, steps * chunks)
    def _(e):
        inner = e % (2 * chunks)
        k_plain, t_plain = e // chunks, e % chunks
        k_pair, t_pair = 2 * (e // (2 * chunks)) + 1 - inner % 2, inner // 2
        k = k_plain + side * (k_pair - k_plain)
        t = t_plain + side * (t_pair - t_plain)

        @pl.when((e == chunks) & (mine >= 1))
        def _():
            send_later()

        @pl.when(e == gather_at)
        def _():
            for q in range(1, rb):
                @pl.loop(0, n_cols)
                def _(j):
                    receive_block(q, j)

                @pl.loop(0, chunks)
                def _(u):
                    load(q, u).wait()

        @pl.when(mine != k)
        def _():
            send_low(0, k, t).wait_recv()
            forward(k, t)
            store_low(k, t).start()

        @pl.when(mine == k + 1)
        def _():
            @pl.when(t == 0)
            def _():
                @pl.loop(0, inv_index)
                def _(j):
                    receive_block(0, j)

            produce(t)

        @pl.when(k == last)
        def _():
            for q in range(1, rb):
                for j in range(steps):
                    acc[q, t] -= jnp.dot(
                        lower[q, j], low[j, t], preferred_element_type=jnp.float32
                    )
                store_rem(q, t).start()

    @pl.loop(0, steps * chunks)
    def _(e):
        k, t = e // chunks, e % chunks
        store_low(k, t).wait()
        for way in range(3):
            @pl.when(goes(way, k))
            def _():
                send_low(way, k, t).wait_send()

    for q in range(rb):
        @pl.loop(0, chunks)
        def _(t):
            store_rem(q, t).wait()

        @pl.loop(0, n_cols)
        def _(j):
            used = mine > j if q == 0 else mine >= -n_rows
            for b in range(len(bits)):
                @pl.when(used & passes(j, b))
                def _():
                    send_block(q, j, b).wait_send()


def on_device(n_rows, n_cols, panel, rhs, inverse):
    rb, block = panel.shape[0], panel.shape[2]
    cols = rhs.shape[3]
    steps = inverse.shape[0]
    assert panel.shape[3] == 1 and n_cols == steps
    assert n_rows % 2 == 0 and steps % 2 == 0 and n_cols & (n_cols - 1) == 0
    width = 128 if cols % 128 == 0 else cols
    chunks = cols // width
    bits = n_cols.bit_length() - 1
    dma = pltpu.SemaphoreType.DMA
    low, remainder = pl.pallas_call(
        functools.partial(kernel, n_rows, n_cols, steps),
        out_shape=(
            jax.ShapeDtypeStruct((steps, block, cols), jnp.bfloat16),
            jax.ShapeDtypeStruct((rb, block, cols), jnp.float32),
        ),
        in_specs=[pl.BlockSpec(memory_space=pl.ANY)] * 3,
        out_specs=(pl.BlockSpec(memory_space=pl.ANY),) * 2,
        scratch_shapes=[
            pltpu.VMEM((steps, chunks, block, width), jnp.bfloat16),
            pltpu.VMEM((rb, chunks, block, width), jnp.float32),
            pltpu.VMEM((block, block), jnp.bfloat16),
            pltpu.VMEM((rb, steps, block, block), jnp.bfloat16),
            dma((rb, chunks)),
            dma((rb,)),
            dma,
            dma((steps, chunks)),
            dma((rb, chunks)),
            dma((3, steps, chunks)),
            dma((steps, chunks)),
            dma((rb, n_cols, bits)),
            dma((rb, n_cols)),
        ],
        compiler_params=pltpu.CompilerParams(
            collective_id=0, has_side_effects=True, vmem_limit_bytes=40 * 2**20
        ),
    )(panel.reshape(rb, block, block), rhs.reshape(rb, block, cols), inverse)
    return low.astype(jnp.float32), remainder.reshape(rhs.shape)


def solution(mesh):
    placed = (P(None, "row", None, "col", None), P(None, "row", None, "col"), P())
    return jax.shard_map(
        functools.partial(on_device, mesh.shape["row"], mesh.shape["col"]),
        mesh=mesh,
        in_specs=placed,
        out_specs=(P(None, None, "col"), P(None, "row", None, "col")),
        check_vma=False,
    )
```

time: 365 us -> 76.7 us (0.21)
  the two profiles are of different devices: /device:TPU:2 before, /device:TPU:0 now
where the time goes in v1:
time: 76.7 us; the launch traced here: 76.5 us
  Pallas kernels  67.5 us (88%)
  local copies, waits for them, and re-layouts  5.72 us (7%)
  other arithmetic  2.6 us (3%)
    pallas_call x1, Pallas kernels, on_device(): pl.pallas_call(functools.partial(kernel, n_rows, n_cols, steps), out_shap...  67.5 us
    unnamed x7, local copies, waits for them, and re-layouts  5.72 us
    convert_element_type x1, other arithmetic, on_device(): return (low.astype(jnp.float32), remainder.reshape(rhs.shape))  2.6 us

profile of v1, /device:TPU:0, one launch (start us, length us, event | category | flops | bytes accessed | tf_op | source)
XLA Modules:
  0.0 76.5 jit_solution(13076317854174397513)
XLA Ops:
  0.6 0.0 copy-start
  0.6 1.6 %copy-done = f32[2,1,512,512]{3,2,1,0:T(8,128)S(1)} copy-done((f32[2,1,512,512]{3,2,1,0:T(8,128)S(1)}, f32[2,1,512,512]{3,2,1,0:T(8,128)}, u32[]{:S(2)}) %copy-start) | copy-done | bytes 2097176
  2.2 0.0 copy-start.1
  2.2 1.6 %copy-done.1 = bf16[4,512,512]{2,1,0:T(8,128)(2,1)S(1)} copy-done((bf16[4,512,512]{2,1,0:T(8,128)(2,1)S(1)}, bf16[4,512,512]{2,1,0:T(8,128)(2,1)}, u32[]{:S(2)}) %copy-start.1) | copy-done | bytes 2097176
  3.8 0.0 copy-start.2
  3.8 1.2 %copy-done.2 = bf16[2,1,512,1,512]{4,2,3,1,0:T(8,128)(2,1)S(1)} copy-done((bf16[2,1,512,1,512]{4,2,3,1,0:T(8,128)(2,1)S(1)}, bf16[2,1,512,1,512]{4,2,3,1,0:T(8,128)(2,1)}, u32[]{:S(2)}) %copy-start.2) | copy-done | bytes 1048600
  5.0 67.5 %shard_map.50 = (bf16[4,512,512]{2,1,0:T(8,128)(2,1)S(1)}, f32[2,512,512]{2,1,0:T(8,128)S(1)}) custom-call(bf16[2,512,512]{2,1,0:T(8,128)(2,1)S(1)} %bitcast.7, f32[2,512,512]{2,1,0:T(8,128)S(1)} %bitcast.5, bf16[4,512,512]{2,1,0:T(8,128)(2,1)S(1)} %copy-done.1), custom_call_target="tpu_custom_call" | custom-call | tf_op jit(solution)/shard_map/pallas_call | solution.py:256
  72.5 2.6 %convert_element_type.3 = f32[4,512,512]{2,1,0:T(8,128)} convert(bf16[4,512,512]{2,1,0:T(8,128)(2,1)S(1)} %get-tuple-element.4) | non-fusion elementwise | flops 1048576 | bytes 6291456 | tf_op jit(solution)/shard_map/convert_element_type | solution.py:283
  75.1 1.3 %copy.7 = f32[2,1,512,512]{3,2,1,0:T(8,128)} copy(f32[2,1,512,512]{3,2,1,0:T(8,128)S(1)} %bitcast.6) | data formatting | bytes 4194304
Async XLA Ops:
  0.6 1.6 %copy-start = (f32[2,1,512,512]{3,2,1,0:T(8,128)S(1)}, f32[2,1,512,512]{3,2,1,0:T(8,128)}, u32[]{:S(2)}) copy-start(f32[2,1,512,512]{3,2,1,0:T(8,128)} %param.4) | copy-start | bytes 6291460
  2.2 1.6 %copy-start.1 = (bf16[4,512,512]{2,1,0:T(8,128)(2,1)S(1)}, bf16[4,512,512]{2,1,0:T(8,128)(2,1)}, u32[]{:S(2)}) copy-start(bf16[4,512,512]{2,1,0:T(8,128)(2,1)} %inverse.1) | copy-start | bytes 6291460
  3.8 1.2 %copy-start.2 = (bf16[2,1,512,1,512]{4,2,3,1,0:T(8,128)(2,1)S(1)}, bf16[2,1,512,1,512]{4,2,3,1,0:T(8,128)(2,1)}, u32[]{:S(2)}) copy-start(bf16[2,1,512,1,512]{4,2,3,1,0:T(8,128)(2,1)} %param.3) | copy-start | bytes 3145732

commit v2 on v1

--- a/solution.py
+++ b/solution.py
@@ -12,11 +12,14 @@
 
 def kernel(
     n_rows, n_cols, steps, panel, rhs, inverse, low_out, rem_out,
-    low, acc, inv, lower,
+    low, natural, base_ref, acc, inv, lower,
     load_sem, own_sem, inv_sem, low_sem, rem_sem, send_sem, recv_sem, psend_sem, precv_sem,
 ):
     rb = acc.shape[0]
-    chunks, width = acc.shape[1], acc.shape[3]
+    tiles, block, width = acc.shape[1:]
+    chunks = low.shape[1]
+    fold = chunks // tiles
+    part, height = width // fold, block // fold
     offset = n_rows - steps
     levels = n_rows // 2
     bits = [1 << b for b in reversed(range(n_cols.bit_length() - 1))]
@@ -43,15 +46,15 @@
     load_inv = pltpu.make_async_copy(inverse.at[inv_index], inv, inv_sem)
 
     def store_low(k, t):
-        return pltpu.make_async_copy(low.at[k, t], low_out.at[k, :, columns(t)], low_sem.at[k, t])
+        return pltpu.make_async_copy(natural.at[k, t], low_out.at[k, :, columns(t)], low_sem.at[k])
 
     def store_rem(q, t):
-        return pltpu.make_async_copy(acc.at[q, t], rem_out.at[q, :, columns(t)], rem_sem.at[q, t])
+        return pltpu.make_async_copy(acc.at[q, t], rem_out.at[q, :, columns(t)], rem_sem.at[q])
 
     def send_low(way, k, t):
         return pltpu.make_async_remote_copy(
             src_ref=low.at[k, t], dst_ref=low.at[k, t],
-            send_sem=send_sem.at[way, k, t], recv_sem=recv_sem.at[k, t],
+            send_sem=send_sem.at[way, k], recv_sem=recv_sem.at[k, t],
             device_id={"row": targets[way]}, device_id_type=MESH,
         )
 
@@ -70,6 +73,35 @@
             def _():
                 send_low(way, k, t).start()
 
+    lane = lax.broadcasted_iota(jnp.int32, (height, width), 1) // part
+
+    def turn(x, shift):
+        return pltpu.roll(x, lax.rem(shift + width, width), 1)
+
+    def spread(p):
+        wide = p.astype(jnp.float32)
+        return jnp.concatenate(
+            [wide] + [pltpu.roll(wide, width - g * part, 1) for g in range(1, fold)], axis=0
+        ).astype(jnp.bfloat16)
+
+    def pack(x):
+        out = x[:height]
+        for g in range(1, fold):
+            moved = pltpu.roll(x[g * height : (g + 1) * height], g * part, 1)
+            out = jnp.where(lane == g, moved, out)
+        return out.astype(jnp.bfloat16)
+
+    def unpack(k, tile):
+        held = [low[k, tile * fold + h].astype(jnp.float32) for h in range(fold)]
+        for g in range(fold):
+            out = held[0] if g == 0 else pltpu.roll(held[0], width - g * part, 1)
+            for h in range(1, fold):
+                shift = (h - g) * part % width
+                moved = held[h] if shift == 0 else pltpu.roll(held[h], shift, 1)
+                out = jnp.where(lane == h, moved, out)
+            natural[k, tile, pl.ds(g * height, height), :] = out.astype(jnp.bfloat16)
+        store_low(k, tile).start()
+
     def send_block(q, j, b):
         return pltpu.make_async_remote_copy(
             src_ref=lower.at[q, j], dst_ref=lower.at[q, j],
@@ -98,14 +130,14 @@
     def _():
         load_inv.start()
 
-    @pl.loop(0, chunks)
+    @pl.loop(0, tiles)
     def _(t):
         load(0, t).start()
 
     for q in range(rb):
         load_own(q).start()
     for q in range(1, rb):
-        @pl.loop(0, chunks)
+        @pl.loop(0, tiles)
         def _(t):
             load(q, t).start()
 
@@ -137,21 +169,32 @@
     def _():
         send_later()
 
-    @pl.loop(0, chunks)
+    @pl.loop(0, tiles)
     def _(t):
         load(0, t).wait()
 
     def produce(t):
+        tile, h = t // fold, t % fold
+        base_ref[...] = turn(acc[0, tile], -h * part)
+
         @pl.loop(0, inv_index)
         def _(j):
-            acc[0, t] -= jnp.dot(lower[0, j], low[j, t], preferred_element_type=jnp.float32)
-
-        low[inv_index, t] = jnp.dot(
-            inv[...], acc[0, t].astype(jnp.bfloat16), preferred_element_type=jnp.float32
-        ).astype(jnp.bfloat16)
+            base_ref[...] -= jnp.dot(
+                lower[0, j], spread(low[j, t]), preferred_element_type=jnp.float32
+            )
+
+        base = base_ref[...]
+        low[inv_index, t] = pack(
+            jnp.dot(inv[...], base.astype(jnp.bfloat16), preferred_element_type=jnp.float32)
+        )
         forward(inv_index, t)
-        store_low(inv_index, t).start()
-        store_rem(0, t).start()
+        group = lax.broadcasted_iota(jnp.int32, (block, width), 1) // part
+        acc[0, tile] = jnp.where(group == h, turn(base, h * part), acc[0, tile])
+
+        @pl.when(h == fold - 1)
+        def _():
+            store_rem(0, tile).start()
+            unpack(inv_index, tile)
 
     @pl.when(mine >= 0)
     def _():
@@ -165,7 +208,7 @@
 
     @pl.when(mine < 0)
     def _():
-        @pl.loop(0, chunks)
+        @pl.loop(0, tiles)
         def _(t):
             store_rem(0, t).start()
 
@@ -191,7 +234,7 @@
                 def _(j):
                     receive_block(q, j)
 
-                @pl.loop(0, chunks)
+                @pl.loop(0, tiles)
                 def _(u):
                     load(q, u).wait()
 
@@ -199,7 +242,10 @@
         def _():
             send_low(0, k, t).wait_recv()
             forward(k, t)
-            store_low(k, t).start()
+
+            @pl.when(t % fold == fold - 1)
+            def _():
+                unpack(k, t // fold)
 
         @pl.when(mine == k + 1)
         def _():
@@ -211,36 +257,36 @@
 
             produce(t)
 
-        @pl.when(k == last)
-        def _():
+        @pl.when((k == last) & (t % fold == fold - 1))
+        def _():
+            tile = t // fold
             for q in range(1, rb):
                 for j in range(steps):
-                    acc[q, t] -= jnp.dot(
-                        lower[q, j], low[j, t], preferred_element_type=jnp.float32
+                    acc[q, tile] -= jnp.dot(
+                        lower[q, j], natural[j, tile], preferred_element_type=jnp.float32
                     )
-                store_rem(q, t).start()
-
-    @pl.loop(0, steps * chunks)
-    def _(e):
-        k, t = e // chunks, e % chunks
-        store_low(k, t).wait()
+                store_rem(q, tile).start()
+
+    for k in range(steps):
         for way in range(3):
             @pl.when(goes(way, k))
             def _():
-                send_low(way, k, t).wait_send()
-
+                pltpu.make_async_remote_copy(
+                    src_ref=low.at[k], dst_ref=low.at[k],
+                    send_sem=send_sem.at[way, k], recv_sem=recv_sem.at[k, 0],
+                    device_id={"row": targets[way]}, device_id_type=MESH,
+                ).wait_send()
     for q in range(rb):
-        @pl.loop(0, chunks)
-        def _(t):
-            store_rem(q, t).wait()
-
-        @pl.loop(0, n_cols)
-        def _(j):
+        for j in range(n_cols):
             used = mine > j if q == 0 else mine >= -n_rows
             for b in range(len(bits)):
                 @pl.when(used & passes(j, b))
                 def _():
                     send_block(q, j, b).wait_send()
+    for k in range(steps):
+        pltpu.make_async_copy(natural.at[k], natural.at[k], low_sem.at[k]).wait()
+    for q in range(rb):
+        pltpu.make_async_copy(acc.at[q], acc.at[q], rem_sem.at[q]).wait()
 
 
 def on_device(n_rows, n_cols, panel, rhs, inverse):
@@ -250,7 +296,8 @@
     assert panel.shape[3] == 1 and n_cols == steps
     assert n_rows % 2 == 0 and steps % 2 == 0 and n_cols & (n_cols - 1) == 0
     width = 128 if cols % 128 == 0 else cols
-    chunks = cols // width
+    tiles = cols // width
+    fold = 2
     bits = n_cols.bit_length() - 1
     dma = pltpu.SemaphoreType.DMA
     low, remainder = pl.pallas_call(
@@ -262,22 +309,24 @@
         in_specs=[pl.BlockSpec(memory_space=pl.ANY)] * 3,
         out_specs=(pl.BlockSpec(memory_space=pl.ANY),) * 2,
         scratch_shapes=[
-            pltpu.VMEM((steps, chunks, block, width), jnp.bfloat16),
-            pltpu.VMEM((rb, chunks, block, width), jnp.float32),
+            pltpu.VMEM((steps, tiles * fold, block // fold, width), jnp.bfloat16),
+            pltpu.VMEM((steps, tiles, block, width), jnp.bfloat16),
+            pltpu.VMEM((block, width), jnp.float32),
+            pltpu.VMEM((rb, tiles, block, width), jnp.float32),
             pltpu.VMEM((block, block), jnp.bfloat16),
             pltpu.VMEM((rb, steps, block, block), jnp.bfloat16),
-            dma((rb, chunks)),
+            dma((rb, tiles)),
             dma((rb,)),
             dma,
-            dma((steps, chunks)),
-            dma((rb, chunks)),
-            dma((3, steps, chunks)),
-            dma((steps, chunks)),
+            dma((steps,)),
+            dma((rb,)),
+            dma((3, steps)),
+            dma((steps, tiles * fold)),
             dma((rb, n_cols, bits)),
             dma((rb, n_cols)),
         ],
         compiler_params=pltpu.CompilerParams(
-            collective_id=0, has_side_effects=True, vmem_limit_bytes=40 * 2**20
+            collective_id=0, has_side_effects=True, vmem_limit_bytes=60 * 2**20
         ),
     )(panel.reshape(rb, block, block), rhs.reshape(rb, block, cols), inverse)
     return low.astype(jnp.float32), remainder.reshape(rhs.shape)

time: 76.7 us -> 77.5 us (1.010)
  local copies, waits for them, and re-layouts: 5.72 us -> 1.32 us
  Pallas kernels: 67.5 us -> 71.1 us
  other arithmetic: 2.6 us -> 4.34 us
    unnamed x7 -> x3, local copies, waits for them, and re-layouts: 5.72 us -> 1.32 us
    pallas_call x1, Pallas kernels: 67.5 us -> 71.1 us  [on_device(): pl.pallas_call(functools.partial(kernel, n_rows, n_cols, steps), out_shap...]
    convert_element_type x1, other arithmetic: 2.6 us -> 4.34 us  [on_device(): return (low.astype(jnp.float32), remainder.reshape(rhs.shape))]
where the time goes in v2:
time: 77.5 us; the launch traced here: 77.4 us
  Pallas kernels  71.1 us (92%)
  other arithmetic  4.34 us (6%)
  local copies, waits for them, and re-layouts  1.32 us (2%)
    pallas_call x1, Pallas kernels, on_device(): pl.pallas_call(functools.partial(kernel, n_rows, n_cols, steps), out_shap...  71.1 us
    convert_element_type x1, other arithmetic, on_device(): return (low.astype(jnp.float32), remainder.reshape(rhs.shape))  4.34 us

profile of v2, /device:TPU:0, one launch (start us, length us, event | category | flops | bytes accessed | tf_op | source)
XLA Modules:
  0.0 77.4 jit_solution(7479257706633483639)
XLA Ops:
  0.6 71.1 %shard_map.50 = (bf16[4,512,512]{2,1,0:T(8,128)(2,1)}, f32[2,512,512]{2,1,0:T(8,128)}) custom-call(bf16[2,512,512]{2,1,0:T(8,128)(2,1)} %bitcast.7, f32[2,512,512]{2,1,0:T(8,128)} %bitcast.5, bf16[4,512,512]{2,1,0:T(8,128)(2,1)} %inverse.1), custom_call_target="tpu_custom_call" | custom-call | tf_op jit(solution)/shard_map/pallas_call | solution.py:303
  71.7 0.0 copy-start
  71.7 4.3 %convert_element_type.3 = f32[4,512,512]{2,1,0:T(8,128)} convert(bf16[4,512,512]{2,1,0:T(8,128)(2,1)} %get-tuple-element.4) | non-fusion elementwise | flops 1048576 | bytes 6291456 | tf_op jit(solution)/shard_map/convert_element_type | solution.py:332
  76.1 0.0 copy-done
  76.1 1.3 %copy.7 = f32[2,1,512,512]{3,2,1,0:T(8,128)} copy(f32[2,1,512,512]{3,2,1,0:T(8,128)S(1)} %bitcast.6) | data formatting | bytes 4194304
Async XLA Ops:
  71.7 4.4 %copy-start = (f32[2,512,512]{2,1,0:T(8,128)S(1)}, f32[2,512,512]{2,1,0:T(8,128)}, u32[]{:S(2)}) copy-start(f32[2,512,512]{2,1,0:T(8,128)} %get-tuple-element.5) | copy-start | bytes 6291460

commit v3 on v2

--- a/solution.py
+++ b/solution.py
@@ -12,7 +12,7 @@
 
 def kernel(
     n_rows, n_cols, steps, panel, rhs, inverse, low_out, rem_out,
-    low, natural, base_ref, acc, inv, lower,
+    low, natural, acc, inv, lower,
     load_sem, own_sem, inv_sem, low_sem, rem_sem, send_sem, recv_sem, psend_sem, precv_sem,
 ):
     rb = acc.shape[0]
@@ -173,17 +173,23 @@
     def _(t):
         load(0, t).wait()
 
-    def produce(t):
+    def produce(t, before):
         tile, h = t // fold, t % fold
-        base_ref[...] = turn(acc[0, tile], -h * part)
-
-        @pl.loop(0, inv_index)
-        def _(j):
-            base_ref[...] -= jnp.dot(
-                lower[0, j], spread(low[j, t]), preferred_element_type=jnp.float32
+
+        @pl.when(h == 0)
+        def _():
+            @pl.loop(0, inv_index - 1)
+            def _(j):
+                acc[0, tile] -= jnp.dot(
+                    lower[0, j], natural[j, tile], preferred_element_type=jnp.float32
+                )
+
+        base = turn(acc[0, tile], -h * part)
+        if before:
+            prev = inv_index - 1
+            base = base - jnp.dot(
+                lower[0, prev], spread(low[prev, t]), preferred_element_type=jnp.float32
             )
-
-        base = base_ref[...]
         low[inv_index, t] = pack(
             jnp.dot(inv[...], base.astype(jnp.bfloat16), preferred_element_type=jnp.float32)
         )
@@ -204,7 +210,7 @@
     def _():
         @pl.loop(0, chunks)
         def _(t):
-            produce(t)
+            produce(t, False)
 
     @pl.when(mine < 0)
     def _():
@@ -212,8 +218,16 @@
         def _(t):
             store_rem(0, t).start()
 
-    gather_at = (steps - 1 - side) * chunks
     last = steps - 1 - side
+    gather_at = last * chunks
+
+    def update(tile, start, stop):
+        for q in range(1, rb):
+            @pl.loop(start, stop)
+            def _(j):
+                acc[q, tile] -= jnp.dot(
+                    lower[q, j], natural[j, tile], preferred_element_type=jnp.float32
+                )
 
     @pl.loop(0, steps * chunks)
     def _(e):
@@ -238,6 +252,12 @@
                 def _(u):
                     load(q, u).wait()
 
+            @pl.when(mine < 0)
+            def _():
+                @pl.loop(0, tiles)
+                def _(u):
+                    update(u, 0, last)
+
         @pl.when(mine != k)
         def _():
             send_low(0, k, t).wait_recv()
@@ -255,17 +275,22 @@
                 def _(j):
                     receive_block(0, j)
 
-            produce(t)
-
-        @pl.when((k == last) & (t % fold == fold - 1))
+            produce(t, True)
+
+        @pl.when((k == last) & (t % fold == fold - 1) & (mine < 0))
         def _():
             tile = t // fold
+            update(tile, last, steps)
             for q in range(1, rb):
-                for j in range(steps):
-                    acc[q, tile] -= jnp.dot(
-                        lower[q, j], natural[j, tile], preferred_element_type=jnp.float32
-                    )
                 store_rem(q, tile).start()
+
+    @pl.when(mine >= 0)
+    def _():
+        @pl.loop(0, tiles)
+        def _(u):
+            update(u, 0, steps)
+            for q in range(1, rb):
+                store_rem(q, u).start()
 
     for k in range(steps):
         for way in range(3):
@@ -306,12 +331,11 @@
             jax.ShapeDtypeStruct((steps, block, cols), jnp.bfloat16),
             jax.ShapeDtypeStruct((rb, block, cols), jnp.float32),
         ),
-        in_specs=[pl.BlockSpec(memory_space=pl.ANY)] * 3,
+        in_specs=[pl.BlockSpec(memory_space=pltpu.HBM)] * 3,
         out_specs=(pl.BlockSpec(memory_space=pl.ANY),) * 2,
         scratch_shapes=[
             pltpu.VMEM((steps, tiles * fold, block // fold, width), jnp.bfloat16),
             pltpu.VMEM((steps, tiles, block, width), jnp.bfloat16),
-            pltpu.VMEM((block, width), jnp.float32),
             pltpu.VMEM((rb, tiles, block, width), jnp.float32),
             pltpu.VMEM((block, block), jnp.bfloat16),
             pltpu.VMEM((rb, steps, block, block), jnp.bfloat16),
@@ -326,9 +350,12 @@
             dma((rb, n_cols)),
         ],
         compiler_params=pltpu.CompilerParams(
-            collective_id=0, has_side_effects=True, vmem_limit_bytes=60 * 2**20
+            collective_id=0, has_side_effects=True, vmem_limit_bytes=40 * 2**20
         ),
-    )(panel.reshape(rb, block, block), rhs.reshape(rb, block, cols), inverse)
+    )(*(
+        pltpu.with_memory_space_constraint(x, pltpu.HBM)
+        for x in (panel.reshape(rb, block, block), rhs.reshape(rb, block, cols), inverse)
+    ))
     return low.astype(jnp.float32), remainder.reshape(rhs.shape)
 
 

time: 77.5 us -> 69.8 us (0.901)
  Pallas kernels: 71.1 us -> 65.1 us
  other arithmetic: 4.34 us -> 2.6 us
    pallas_call x1, Pallas kernels: 71.1 us -> 65.1 us  [on_device(): pl.pallas_call(functools.partial(kernel, n_rows, n_cols, steps), out_shap...]
    convert_element_type x1, other arithmetic: 4.34 us -> 2.6 us  [on_device(): return (low.astype(jnp.float32), remainder.reshape(rhs.shape))]
where the time goes in v3:
time: 69.8 us; the launch traced here: 69.7 us
  Pallas kernels  65.1 us (93%)
  other arithmetic  2.6 us (4%)
  local copies, waits for them, and re-layouts  1.32 us (2%)
    pallas_call x1, Pallas kernels, on_device(): pl.pallas_call(functools.partial(kernel, n_rows, n_cols, steps), out_shap...  65.1 us
    convert_element_type x1, other arithmetic, on_device(): return (low.astype(jnp.float32), remainder.reshape(rhs.shape))  2.6 us

profile of v3, /device:TPU:0, one launch (start us, length us, event | category | flops | bytes accessed | tf_op | source)
XLA Modules:
  0.0 69.7 jit_solution(13640120717698905281)
XLA Ops:
  0.6 65.1 %shard_map.50 = (bf16[4,512,512]{2,1,0:T(8,128)(2,1)S(1)}, f32[2,512,512]{2,1,0:T(8,128)S(1)}) custom-call(bf16[2,512,512]{2,1,0:T(8,128)(2,1)} %bitcast.7, f32[2,512,512]{2,1,0:T(8,128)} %bitcast.6, bf16[4,512,512]{2,1,0:T(8,128)(2,1)} %inverse.1), custom_call_target="tpu_custom_call" | custom-call | tf_op jit(solution)/shard_map/pallas_call | solution.py:328
  65.8 2.6 %convert_element_type.3 = f32[4,512,512]{2,1,0:T(8,128)} convert(bf16[4,512,512]{2,1,0:T(8,128)(2,1)S(1)} %get-tuple-element.4) | non-fusion elementwise | flops 1048576 | bytes 6291456 | tf_op jit(solution)/shard_map/convert_element_type | solution.py:359
  68.4 1.3 %copy.7 = f32[2,1,512,512]{3,2,1,0:T(8,128)} copy(f32[2,1,512,512]{3,2,1,0:T(8,128)S(1)} %bitcast.5) | data formatting | bytes 4194304

commit v4 on v3

--- a/solution.py
+++ b/solution.py
@@ -165,7 +165,7 @@
         for q in range(1, rb):
             send_own(q)
 
-    @pl.when(mine < 1)
+    @pl.when(mine < 0)
     def _():
         send_later()
 
@@ -212,6 +212,8 @@
         def _(t):
             produce(t, False)
 
+        send_later()
+
     @pl.when(mine < 0)
     def _():
         @pl.loop(0, tiles)
@@ -220,6 +222,16 @@
 
     last = steps - 1 - side
     gather_at = last * chunks
+
+    def gather():
+        for q in range(1, rb):
+            @pl.loop(0, n_cols)
+            def _(j):
+                receive_block(q, j)
+
+            @pl.loop(0, tiles)
+            def _(u):
+                load(q, u).wait()
 
     def update(tile, start, stop):
         for q in range(1, rb):
@@ -237,26 +249,17 @@
         k = k_plain + side * (k_pair - k_plain)
         t = t_plain + side * (t_pair - t_plain)
 
-        @pl.when((e == chunks) & (mine >= 1))
+        @pl.when((e == (mine + side) * chunks) & (mine >= 1))
         def _():
             send_later()
 
-        @pl.when(e == gather_at)
-        def _():
-            for q in range(1, rb):
-                @pl.loop(0, n_cols)
-                def _(j):
-                    receive_block(q, j)
-
-                @pl.loop(0, tiles)
-                def _(u):
-                    load(q, u).wait()
-
-            @pl.when(mine < 0)
-            def _():
-                @pl.loop(0, tiles)
-                def _(u):
-                    update(u, 0, last)
+        @pl.when((e == gather_at) & (mine < 0))
+        def _():
+            gather()
+
+            @pl.loop(0, tiles)
+            def _(u):
+                update(u, 0, last)
 
         @pl.when(mine != k)
         def _():
@@ -284,8 +287,14 @@
             for q in range(1, rb):
                 store_rem(q, tile).start()
 
+    @pl.when(mine == steps - 1)
+    def _():
+        send_later()
+
     @pl.when(mine >= 0)
     def _():
+        gather()
+
         @pl.loop(0, tiles)
         def _(u):
             update(u, 0, steps)

time: 69.8 us -> 64.5 us (0.924)
  the two profiles are of different devices: /device:TPU:0 before, /device:TPU:28 now
where the time goes in v4:
time: 64.5 us; the launch traced here: 64.4 us
  Pallas kernels  59.8 us (93%)
  other arithmetic  2.6 us (4%)
  local copies, waits for them, and re-layouts  1.32 us (2%)
    pallas_call x1, Pallas kernels, on_device(): pl.pallas_call(functools.partial(kernel, n_rows, n_cols, steps), out_shap...  59.8 us
    convert_element_type x1, other arithmetic, on_device(): return (low.astype(jnp.float32), remainder.reshape(rhs.shape))  2.6 us
    unnamed x1, local copies, waits for them, and re-layouts  1.32 us

profile of v4, /device:TPU:28, one launch (start us, length us, event | category | flops | bytes accessed | tf_op | source)
XLA Modules:
  0.0 64.4 jit_solution(10685711115682911446)
XLA Ops:
  0.6 59.8 %shard_map.50 = (bf16[4,512,512]{2,1,0:T(8,128)(2,1)S(1)}, f32[2,512,512]{2,1,0:T(8,128)S(1)}) custom-call(bf16[2,512,512]{2,1,0:T(8,128)(2,1)} %bitcast.7, f32[2,512,512]{2,1,0:T(8,128)} %bitcast.6, bf16[4,512,512]{2,1,0:T(8,128)(2,1)} %inverse.1), custom_call_target="tpu_custom_call" | custom-call | tf_op jit(solution)/shard_map/pallas_call | solution.py:337
  60.4 2.6 %convert_element_type.3 = f32[4,512,512]{2,1,0:T(8,128)} convert(bf16[4,512,512]{2,1,0:T(8,128)(2,1)S(1)} %get-tuple-element.4) | non-fusion elementwise | flops 1048576 | bytes 6291456 | tf_op jit(solution)/shard_map/convert_element_type | solution.py:368
  63.0 1.3 %copy.7 = f32[2,1,512,512]{3,2,1,0:T(8,128)} copy(f32[2,1,512,512]{3,2,1,0:T(8,128)S(1)} %bitcast.5) | data formatting | bytes 4194304

commit v5 on v4

--- a/solution.py
+++ b/solution.py
@@ -68,8 +68,8 @@
         return same & (level < levels - 1) & (level >= home)
 
     def forward(k, t):
-        for way in range(3):
-            @pl.when(goes(way, k))
+        for way, when in ((0, side == 0), (2, True), (1, True), (0, side == 1)):
+            @pl.when(goes(way, k) & when)
             def _():
                 send_low(way, k, t).start()
 
@@ -111,8 +111,22 @@
 
     def send_own(q):
         load_own(q).wait()
-        for b in range(len(bits)):
+        for b in reversed(range(len(bits))):
             send_block(q, col, b).start()
+
+    def send_piece(p):
+        rows = pl.ds(pl.multiple_of(p * (block // chunks), block // chunks), block // chunks)
+        for q in range(1, rb):
+            @pl.when(p == 0)
+            def _():
+                load_own(q).wait()
+
+            for b in reversed(range(len(bits))):
+                pltpu.make_async_remote_copy(
+                    src_ref=lower.at[q, col, rows], dst_ref=lower.at[q, col, rows],
+                    send_sem=psend_sem.at[q, col, b], recv_sem=precv_sem.at[q, col],
+                    device_id={"col": flip(bits[b])}, device_id_type=MESH,
+                ).start()
 
     def passes(j, b):
         return (col % (2 * bits[b])) == (j % (2 * bits[b]))
@@ -121,7 +135,7 @@
         @pl.when(col != j)
         def _():
             send_block(q, j, 0).wait_recv()
-            for b in range(len(bits)):
+            for b in reversed(range(len(bits))):
                 @pl.when(passes(j, b))
                 def _():
                     send_block(q, j, b).start()
@@ -249,11 +263,23 @@
         k = k_plain + side * (k_pair - k_plain)
         t = t_plain + side * (t_pair - t_plain)
 
-        @pl.when((e == (mine + side) * chunks) & (mine >= 1))
+        @pl.when((e == mine * chunks) & (mine >= 1) & (side == 0))
         def _():
             send_later()
 
-        @pl.when((e == gather_at) & (mine < 0))
+        begin = (mine + 1) * chunks
+
+        @pl.when((mine >= 1) & (side == 1) & (e == begin))
+        def _():
+            @pl.loop(0, chunks // 2)
+            def _(p):
+                send_piece(p)
+
+        @pl.when((mine >= 1) & (side == 1) & (e > begin) & (e <= begin + chunks // 2))
+        def _():
+            send_piece(e - begin - 1 + chunks // 2)
+
+        @pl.when((e == gather_at) & ((mine < 0) | (side == 0)))
         def _():
             gather()
 
@@ -280,18 +306,18 @@
 
             produce(t, True)
 
-        @pl.when((k == last) & (t % fold == fold - 1) & (mine < 0))
+            @pl.when(mine == steps - 1)
+            def _():
+                send_piece(t)
+
+        @pl.when((k == last) & (t % fold == fold - 1) & ((mine < 0) | (side == 0)))
         def _():
             tile = t // fold
             update(tile, last, steps)
             for q in range(1, rb):
                 store_rem(q, tile).start()
 
-    @pl.when(mine == steps - 1)
-    def _():
-        send_later()
-
-    @pl.when(mine >= 0)
+    @pl.when((mine >= 0) & (side == 1))
     def _():
         gather()
 

time: 64.5 us -> 60.3 us (0.935)
  the two profiles are of different devices: /device:TPU:28 before, /device:TPU:2 now
where the time goes in v5:
time: 60.3 us; the launch traced here: 60.2 us
  Pallas kernels  55.6 us (92%)
  other arithmetic  2.6 us (4%)
  local copies, waits for them, and re-layouts  1.32 us (2%)
  between operations  0.64 us (1%)
    pallas_call x1, Pallas kernels, on_device(): pl.pallas_call(functools.partial(kernel, n_rows, n_cols, steps), out_shap...  55.6 us
    convert_element_type x1, other arithmetic, on_device(): return (low.astype(jnp.float32), remainder.reshape(rhs.shape))  2.6 us
    unnamed x1, local copies, waits for them, and re-layouts  1.32 us

profile of v5, /device:TPU:2, one launch (start us, length us, event | category | flops | bytes accessed | tf_op | source)
XLA Modules:
  0.0 60.2 jit_solution(4485652487621572556)
XLA Ops:
  0.6 55.6 %shard_map.50 = (bf16[4,512,512]{2,1,0:T(8,128)(2,1)S(1)}, f32[2,512,512]{2,1,0:T(8,128)S(1)}) custom-call(bf16[2,512,512]{2,1,0:T(8,128)(2,1)} %bitcast.7, f32[2,512,512]{2,1,0:T(8,128)} %bitcast.6, bf16[4,512,512]{2,1,0:T(8,128)(2,1)} %inverse.1), custom_call_target="tpu_custom_call" | custom-call | tf_op jit(solution)/shard_map/pallas_call | solution.py:363
  56.2 2.6 %convert_element_type.3 = f32[4,512,512]{2,1,0:T(8,128)} convert(bf16[4,512,512]{2,1,0:T(8,128)(2,1)S(1)} %get-tuple-element.4) | non-fusion elementwise | flops 1048576 | bytes 6291456 | tf_op jit(solution)/shard_map/convert_element_type | solution.py:394
  58.8 1.3 %copy.7 = f32[2,1,512,512]{3,2,1,0:T(8,128)} copy(f32[2,1,512,512]{3,2,1,0:T(8,128)S(1)} %bitcast.5) | data formatting | bytes 4194304

commit v6 on v5

--- a/solution.py
+++ b/solution.py
@@ -131,14 +131,25 @@
     def passes(j, b):
         return (col % (2 * bits[b])) == (j % (2 * bits[b]))
 
-    def receive_block(q, j):
-        @pl.when(col != j)
-        def _():
-            send_block(q, j, 0).wait_recv()
-            for b in reversed(range(len(bits))):
-                @pl.when(passes(j, b))
-                def _():
-                    send_block(q, j, b).start()
+    def receive_blocks(q, count):
+        def duty(j):
+            return (col != j) & passes(j, len(bits) - 1)
+
+        @pl.loop(0, count)
+        def _(j):
+            @pl.when(duty(j))
+            def _():
+                send_block(q, j, 0).wait_recv()
+                for b in reversed(range(len(bits))):
+                    @pl.when(passes(j, b))
+                    def _():
+                        send_block(q, j, b).start()
+
+        @pl.loop(0, count)
+        def _(j):
+            @pl.when((col != j) & jnp.logical_not(duty(j)))
+            def _():
+                send_block(q, j, 0).wait_recv()
 
     @pl.when(mine >= 0)
     def _():
@@ -190,7 +201,7 @@
     def produce(t, before):
         tile, h = t // fold, t % fold
 
-        @pl.when(h == 0)
+        @pl.when((h == 0) & (side == 0))
         def _():
             @pl.loop(0, inv_index - 1)
             def _(j):
@@ -239,9 +250,7 @@
 
     def gather():
         for q in range(1, rb):
-            @pl.loop(0, n_cols)
-            def _(j):
-                receive_block(q, j)
+            receive_blocks(q, n_cols)
 
             @pl.loop(0, tiles)
             def _(u):
@@ -296,13 +305,23 @@
             def _():
                 unpack(k, t // fold)
 
+        @pl.when((side == 1) & (k % 2 == 0) & (k + 3 <= mine) & (t % fold == fold - 1))
+        def _():
+            @pl.when((k == 0) & (t == fold - 1))
+            def _():
+                receive_blocks(0, inv_index)
+
+            @pl.loop(k, k + 2)
+            def _(j):
+                acc[0, t // fold] -= jnp.dot(
+                    lower[0, j], natural[j, t // fold], preferred_element_type=jnp.float32
+                )
+
         @pl.when(mine == k + 1)
         def _():
-            @pl.when(t == 0)
-            def _():
-                @pl.loop(0, inv_index)
-                def _(j):
-                    receive_block(0, j)
+            @pl.when((t == 0) & ((side == 0) | (mine == 1)))
+            def _():
+                receive_blocks(0, inv_index)
 
             produce(t, True)
 

time: 60.3 us -> 57.5 us (0.954)
  Pallas kernels: 55.6 us -> 52.8 us
    pallas_call x1, Pallas kernels: 55.6 us -> 52.8 us  [on_device(): pl.pallas_call(functools.partial(kernel, n_rows, n_cols, steps), out_shap...]
where the time goes in v6:
time: 57.5 us; the launch traced here: 57.4 us
  Pallas kernels  52.8 us (92%)
  other arithmetic  2.6 us (5%)
  local copies, waits for them, and re-layouts  1.32 us (2%)
  between operations  0.64 us (1%)
    pallas_call x1, Pallas kernels, on_device(): pl.pallas_call(functools.partial(kernel, n_rows, n_cols, steps), out_shap...  52.8 us
    convert_element_type x1, other arithmetic, on_device(): return (low.astype(jnp.float32), remainder.reshape(rhs.shape))  2.6 us
    unnamed x1, local copies, waits for them, and re-layouts  1.32 us

profile of v6, /device:TPU:2, one launch (start us, length us, event | category | flops | bytes accessed | tf_op | source)
XLA Modules:
  0.0 57.4 jit_solution(12917510270769587697)
XLA Ops:
  0.6 52.8 %shard_map.50 = (bf16[4,512,512]{2,1,0:T(8,128)(2,1)S(1)}, f32[2,512,512]{2,1,0:T(8,128)S(1)}) custom-call(bf16[2,512,512]{2,1,0:T(8,128)(2,1)} %bitcast.7, f32[2,512,512]{2,1,0:T(8,128)} %bitcast.6, bf16[4,512,512]{2,1,0:T(8,128)(2,1)} %inverse.1), custom_call_target="tpu_custom_call" | custom-call | tf_op jit(solution)/shard_map/pallas_call | solution.py:382
  53.5 2.6 %convert_element_type.3 = f32[4,512,512]{2,1,0:T(8,128)} convert(bf16[4,512,512]{2,1,0:T(8,128)(2,1)S(1)} %get-tuple-element.4) | non-fusion elementwise | flops 1048576 | bytes 6291456 | tf_op jit(solution)/shard_map/convert_element_type | solution.py:413
  56.1 1.3 %copy.7 = f32[2,1,512,512]{3,2,1,0:T(8,128)} copy(f32[2,1,512,512]{3,2,1,0:T(8,128)S(1)} %bitcast.5) | data formatting | bytes 4194304

commit v7 on v6

--- a/solution.py
+++ b/solution.py
@@ -173,11 +173,38 @@
             pl.semaphore_signal(barrier, inc=1, device_id={"row": targets[way]}, device_id_type=MESH)
     for bit in bits:
         pl.semaphore_signal(barrier, inc=1, device_id={"col": flip(bit)}, device_id_type=MESH)
+    @pl.when(mine == 0)
+    def _():
+        load_inv.wait()
+
+        @pl.loop(0, tiles)
+        def _(t):
+            load(0, t).wait()
+            fresh = jnp.dot(
+                inv[...], acc[0, t].astype(jnp.bfloat16), preferred_element_type=jnp.float32
+            )
+            natural[0, t] = fresh.astype(jnp.bfloat16)
+            for h in range(fold):
+                low[0, t * fold + h] = pack(
+                    fresh if h == 0 else pltpu.roll(fresh, width - h * part, 1)
+                )
+
     pl.semaphore_wait(
         barrier,
         1 + len(bits) + jnp.minimum(level, 1) + jnp.minimum(levels - 1 - level, 1),
     )
 
+    @pl.when(mine == 0)
+    def _():
+        @pl.loop(0, chunks)
+        def _(t):
+            forward(0, t)
+
+        @pl.loop(0, tiles)
+        def _(t):
+            store_low(0, t).start()
+            store_rem(0, t).start()
+
     @pl.when(mine > col)
     def _():
         send_own(0)
@@ -190,15 +217,26 @@
         for q in range(1, rb):
             send_own(q)
 
-    @pl.when(mine < 0)
+    @pl.when(mine <= 0)
     def _():
         send_later()
 
-    @pl.loop(0, tiles)
-    def _(t):
-        load(0, t).wait()
-
-    def produce(t, before):
+    early = (mine >= 1) & (col >= mine) & (col >= n_cols // 2)
+    half = chunks // 2
+
+    @pl.when(early)
+    def _():
+        @pl.loop(0, half)
+        def _(p):
+            send_piece(p)
+
+    @pl.when(mine != 0)
+    def _():
+        @pl.loop(0, tiles)
+        def _(t):
+            load(0, t).wait()
+
+    def produce(t):
         tile, h = t // fold, t % fold
 
         @pl.when((h == 0) & (side == 0))
@@ -210,11 +248,10 @@
                 )
 
         base = turn(acc[0, tile], -h * part)
-        if before:
-            prev = inv_index - 1
-            base = base - jnp.dot(
-                lower[0, prev], spread(low[prev, t]), preferred_element_type=jnp.float32
-            )
+        prev = inv_index - 1
+        base = base - jnp.dot(
+            lower[0, prev], spread(low[prev, t]), preferred_element_type=jnp.float32
+        )
         low[inv_index, t] = pack(
             jnp.dot(inv[...], base.astype(jnp.bfloat16), preferred_element_type=jnp.float32)
         )
@@ -227,17 +264,9 @@
             store_rem(0, tile).start()
             unpack(inv_index, tile)
 
-    @pl.when(mine >= 0)
+    @pl.when(mine >= 1)
     def _():
         load_inv.wait()
-
-    @pl.when(mine == 0)
-    def _():
-        @pl.loop(0, chunks)
-        def _(t):
-            produce(t, False)
-
-        send_later()
 
     @pl.when(mine < 0)
     def _():
@@ -274,19 +303,22 @@
 
         @pl.when((e == mine * chunks) & (mine >= 1) & (side == 0))
         def _():
-            send_later()
-
-        begin = (mine + 1) * chunks
-
-        @pl.when((mine >= 1) & (side == 1) & (e == begin))
-        def _():
-            @pl.loop(0, chunks // 2)
+            @pl.loop(jnp.where(early, half, 0), chunks)
             def _(p):
                 send_piece(p)
 
-        @pl.when((mine >= 1) & (side == 1) & (e > begin) & (e <= begin + chunks // 2))
-        def _():
-            send_piece(e - begin - 1 + chunks // 2)
+        begin = (mine + 1) * chunks
+        late = (mine >= 1) & (side == 1) & (mine < steps - 1)
+
+        @pl.when(late & jnp.logical_not(early) & (e == begin))
+        def _():
+            @pl.loop(0, half)
+            def _(p):
+                send_piece(p)
+
+        @pl.when(late & (e > begin) & (e <= begin + chunks - half))
+        def _():
+            send_piece(e - begin - 1 + half)
 
         @pl.when((e == gather_at) & ((mine < 0) | (side == 0)))
         def _():
@@ -323,9 +355,9 @@
             def _():
                 receive_blocks(0, inv_index)
 
-            produce(t, True)
-
-            @pl.when(mine == steps - 1)
+            produce(t)
+
+            @pl.when((mine == steps - 1) & (jnp.logical_not(early) | (t >= half)))
             def _():
                 send_piece(t)
 

time: 57.5 us -> 57.8 us (level)
  no operation moved by 1% of the time
where the time goes in v7:
time: 57.8 us; the launch traced here: 57.7 us
  Pallas kernels  53.1 us (92%)
  other arithmetic  2.6 us (4%)
  local copies, waits for them, and re-layouts  1.32 us (2%)
  between operations  0.64 us (1%)
    pallas_call x1, Pallas kernels, on_device(): pl.pallas_call(functools.partial(kernel, n_rows, n_cols, steps), out_shap...  53.1 us
    convert_element_type x1, other arithmetic, on_device(): return (low.astype(jnp.float32), remainder.reshape(rhs.shape))  2.6 us
    unnamed x1, local copies, waits for them, and re-layouts  1.32 us

profile of v7, /device:TPU:2, one launch (start us, length us, event | category | flops | bytes accessed | tf_op | source)
XLA Modules:
  0.0 57.7 jit_solution(18350101075319916836)
XLA Ops:
  0.6 53.1 %shard_map.50 = (bf16[4,512,512]{2,1,0:T(8,128)(2,1)S(1)}, f32[2,512,512]{2,1,0:T(8,128)S(1)}) custom-call(bf16[2,512,512]{2,1,0:T(8,128)(2,1)} %bitcast.7, f32[2,512,512]{2,1,0:T(8,128)} %bitcast.6, bf16[4,512,512]{2,1,0:T(8,128)(2,1)} %inverse.1), custom_call_target="tpu_custom_call" | custom-call | tf_op jit(solution)/shard_map/pallas_call | solution.py:414
  53.8 2.6 %convert_element_type.3 = f32[4,512,512]{2,1,0:T(8,128)} convert(bf16[4,512,512]{2,1,0:T(8,128)(2,1)S(1)} %get-tuple-element.4) | non-fusion elementwise | flops 1048576 | bytes 6291456 | tf_op jit(solution)/shard_map/convert_element_type | solution.py:445
  56.4 1.3 %copy.7 = f32[2,1,512,512]{3,2,1,0:T(8,128)} copy(f32[2,1,512,512]{3,2,1,0:T(8,128)S(1)} %bitcast.5) | data formatting | bytes 4194304

commit v8 on v7

--- a/solution.py
+++ b/solution.py
@@ -51,10 +51,11 @@
     def store_rem(q, t):
         return pltpu.make_async_copy(acc.at[q, t], rem_out.at[q, :, columns(t)], rem_sem.at[q])
 
-    def send_low(way, k, t):
+    def send_low(way, k, t, p):
+        rows = pl.ds(p * (height // 2), height // 2)
         return pltpu.make_async_remote_copy(
-            src_ref=low.at[k, t], dst_ref=low.at[k, t],
-            send_sem=send_sem.at[way, k], recv_sem=recv_sem.at[k, t],
+            src_ref=low.at[k, t, rows], dst_ref=low.at[k, t, rows],
+            send_sem=send_sem.at[way, k], recv_sem=recv_sem.at[k, t, p],
             device_id={"row": targets[way]}, device_id_type=MESH,
         )
 
@@ -68,10 +69,14 @@
         return same & (level < levels - 1) & (level >= home)
 
     def forward(k, t):
+        for p in range(2):
+            forward_half(k, t, p)
+
+    def forward_half(k, t, p):
         for way, when in ((0, side == 0), (2, True), (1, True), (0, side == 1)):
             @pl.when(goes(way, k) & when)
             def _():
-                send_low(way, k, t).start()
+                send_low(way, k, t, p).start()
 
     lane = lax.broadcasted_iota(jnp.int32, (height, width), 1) // part
 
@@ -173,21 +178,21 @@
             pl.semaphore_signal(barrier, inc=1, device_id={"row": targets[way]}, device_id_type=MESH)
     for bit in bits:
         pl.semaphore_signal(barrier, inc=1, device_id={"col": flip(bit)}, device_id_type=MESH)
+    def solve_first(t):
+        load(0, t).wait()
+        fresh = jnp.dot(
+            inv[...], acc[0, t].astype(jnp.bfloat16), preferred_element_type=jnp.float32
+        )
+        natural[0, t] = fresh.astype(jnp.bfloat16)
+        for h in range(fold):
+            low[0, t * fold + h] = pack(
+                fresh if h == 0 else pltpu.roll(fresh, width - h * part, 1)
+            )
+
     @pl.when(mine == 0)
     def _():
         load_inv.wait()
-
-        @pl.loop(0, tiles)
-        def _(t):
-            load(0, t).wait()
-            fresh = jnp.dot(
-                inv[...], acc[0, t].astype(jnp.bfloat16), preferred_element_type=jnp.float32
-            )
-            natural[0, t] = fresh.astype(jnp.bfloat16)
-            for h in range(fold):
-                low[0, t * fold + h] = pack(
-                    fresh if h == 0 else pltpu.roll(fresh, width - h * part, 1)
-                )
+        solve_first(0)
 
     pl.semaphore_wait(
         barrier,
@@ -196,12 +201,14 @@
 
     @pl.when(mine == 0)
     def _():
-        @pl.loop(0, chunks)
-        def _(t):
-            forward(0, t)
-
         @pl.loop(0, tiles)
         def _(t):
+            @pl.when(t > 0)
+            def _():
+                solve_first(t)
+
+            for h in range(fold):
+                forward(0, t * fold + h)
             store_low(0, t).start()
             store_rem(0, t).start()
 
@@ -330,8 +337,9 @@
 
         @pl.when(mine != k)
         def _():
-            send_low(0, k, t).wait_recv()
-            forward(k, t)
+            for p in range(2):
+                send_low(0, k, t, p).wait_recv()
+                forward_half(k, t, p)
 
             @pl.when(t % fold == fold - 1)
             def _():
@@ -384,7 +392,7 @@
             def _():
                 pltpu.make_async_remote_copy(
                     src_ref=low.at[k], dst_ref=low.at[k],
-                    send_sem=send_sem.at[way, k], recv_sem=recv_sem.at[k, 0],
+                    send_sem=send_sem.at[way, k], recv_sem=recv_sem.at[k, 0, 0],
                     device_id={"row": targets[way]}, device_id_type=MESH,
                 ).wait_send()
     for q in range(rb):
@@ -431,7 +439,7 @@
             dma((steps,)),
             dma((rb,)),
             dma((3, steps)),
-            dma((steps, tiles * fold)),
+            dma((steps, tiles * fold, 2)),
             dma((rb, n_cols, bits)),
             dma((rb, n_cols)),
         ],

time: 57.8 us -> 57 us (0.986); the launches traced: 57.7 us -> 56.1 us
  Pallas kernels: 53.1 us -> 51.6 us
    pallas_call x1, Pallas kernels: 53.1 us -> 51.6 us  [on_device(): pl.pallas_call(functools.partial(kernel, n_rows, n_cols, steps), out_shap...]
where the time goes in v8:
time: 57 us; the launch traced here: 56.1 us
  Pallas kernels  51.6 us (91%)
  other arithmetic  2.6 us (5%)
  local copies, waits for them, and re-layouts  1.32 us (2%)
  between operations  0.64 us (1%)
    pallas_call x1, Pallas kernels, on_device(): pl.pallas_call(functools.partial(kernel, n_rows, n_cols, steps), out_shap...  51.6 us
    convert_element_type x1, other arithmetic, on_device(): return (low.astype(jnp.float32), remainder.reshape(rhs.shape))  2.6 us
    unnamed x1, local copies, waits for them, and re-layouts  1.32 us

profile of v8, /device:TPU:2, one launch (start us, length us, event | category | flops | bytes accessed | tf_op | source)
XLA Modules:
  0.0 56.1 jit_solution(8261020667507368074)
XLA Ops:
  0.6 51.6 %shard_map.50 = (bf16[4,512,512]{2,1,0:T(8,128)(2,1)S(1)}, f32[2,512,512]{2,1,0:T(8,128)S(1)}) custom-call(bf16[2,512,512]{2,1,0:T(8,128)(2,1)} %bitcast.7, f32[2,512,512]{2,1,0:T(8,128)} %bitcast.6, bf16[4,512,512]{2,1,0:T(8,128)(2,1)} %inverse.1), custom_call_target="tpu_custom_call" | custom-call | tf_op jit(solution)/shard_map/pallas_call | solution.py:422
  52.2 2.6 %convert_element_type.3 = f32[4,512,512]{2,1,0:T(8,128)} convert(bf16[4,512,512]{2,1,0:T(8,128)(2,1)S(1)} %get-tuple-element.4) | non-fusion elementwise | flops 1048576 | bytes 6291456 | tf_op jit(solution)/shard_map/convert_element_type | solution.py:453
  54.8 1.3 %copy.7 = f32[2,1,512,512]{3,2,1,0:T(8,128)} copy(f32[2,1,512,512]{3,2,1,0:T(8,128)S(1)} %bitcast.5) | data formatting | bytes 4194304

commit v9 on v8

--- a/solution.py
+++ b/solution.py
@@ -282,7 +282,8 @@
             store_rem(0, t).start()
 
     last = steps - 1 - side
-    gather_at = last * chunks
+    first = steps - 2
+    gather_at = first * chunks
 
     def gather():
         for q in range(1, rb):
@@ -333,7 +334,7 @@
 
             @pl.loop(0, tiles)
             def _(u):
-                update(u, 0, last)
+                update(u, 0, first)
 
         @pl.when(mine != k)
         def _():
@@ -369,12 +370,17 @@
             def _():
                 send_piece(t)
 
-        @pl.when((k == last) & (t % fold == fold - 1) & ((mine < 0) | (side == 0)))
+        @pl.when(
+            (k >= first) & ((side == 0) | ((k == last) & (mine < 0))) & (t % fold == fold - 1)
+        )
         def _():
             tile = t // fold
-            update(tile, last, steps)
-            for q in range(1, rb):
-                store_rem(q, tile).start()
+            update(tile, first + (1 - side) * (k - first), steps - (1 - side) * (steps - 1 - k))
+
+            @pl.when(k == last)
+            def _():
+                for q in range(1, rb):
+                    store_rem(q, tile).start()
 
     @pl.when((mine >= 0) & (side == 1))
     def _():

time: 57 us -> 59.3 us (1.040); the launches traced: 56.1 us -> 59.2 us
  Pallas kernels: 51.6 us -> 54.6 us
    pallas_call x1, Pallas kernels: 51.6 us -> 54.6 us  [on_device(): pl.pallas_call(functools.partial(kernel, n_rows, n_cols, steps), out_shap...]
where the time goes in v9:
time: 59.3 us; the launch traced here: 59.2 us
  Pallas kernels  54.6 us (92%)
  other arithmetic  2.6 us (4%)
  local copies, waits for them, and re-layouts  1.32 us (2%)
  between operations  0.64 us (1%)
    pallas_call x1, Pallas kernels, on_device(): pl.pallas_call(functools.partial(kernel, n_rows, n_cols, steps), out_shap...  54.6 us
    convert_element_type x1, other arithmetic, on_device(): return (low.astype(jnp.float32), remainder.reshape(rhs.shape))  2.6 us
    unnamed x1, local copies, waits for them, and re-layouts  1.32 us

profile of v9, /device:TPU:2, one launch (start us, length us, event | category | flops | bytes accessed | tf_op | source)
XLA Modules:
  0.0 59.2 jit_solution(11461165604503413098)
XLA Ops:
  0.6 54.6 %shard_map.50 = (bf16[4,512,512]{2,1,0:T(8,128)(2,1)S(1)}, f32[2,512,512]{2,1,0:T(8,128)S(1)}) custom-call(bf16[2,512,512]{2,1,0:T(8,128)(2,1)} %bitcast.7, f32[2,512,512]{2,1,0:T(8,128)} %bitcast.6, bf16[4,512,512]{2,1,0:T(8,128)(2,1)} %inverse.1), custom_call_target="tpu_custom_call" | custom-call | tf_op jit(solution)/shard_map/pallas_call | solution.py:428
  55.3 2.6 %convert_element_type.3 = f32[4,512,512]{2,1,0:T(8,128)} convert(bf16[4,512,512]{2,1,0:T(8,128)(2,1)S(1)} %get-tuple-element.4) | non-fusion elementwise | flops 1048576 | bytes 6291456 | tf_op jit(solution)/shard_map/convert_element_type | solution.py:459
  57.9 1.3 %copy.7 = f32[2,1,512,512]{3,2,1,0:T(8,128)} copy(f32[2,1,512,512]{3,2,1,0:T(8,128)S(1)} %bitcast.5) | data formatting | bytes 4194304

commit v10 on v8

--- a/solution.py
+++ b/solution.py
@@ -281,6 +281,7 @@
         def _(t):
             store_rem(0, t).start()
 
+    ahead = min(2, chunks)
     last = steps - 1 - side
     gather_at = last * chunks
 
@@ -304,7 +305,20 @@
     def _(e):
         inner = e % (2 * chunks)
         k_plain, t_plain = e // chunks, e % chunks
-        k_pair, t_pair = 2 * (e // (2 * chunks)) + 1 - inner % 2, inner // 2
+        middle = inner - ahead
+        head = inner < ahead
+        tail = inner >= 2 * chunks - ahead
+        own = head | (jnp.logical_not(tail) & (middle % 2 == 0))
+        k_pair = 2 * (e // (2 * chunks)) + jnp.where(own, 1, 0)
+        t_pair = jnp.where(
+            head,
+            inner,
+            jnp.where(
+                tail,
+                inner - chunks,
+                jnp.where(own, ahead + middle // 2, middle // 2),
+            ),
+        )
         k = k_plain + side * (k_pair - k_plain)
         t = t_plain + side * (t_pair - t_plain)
 

time: 57 us -> 57.9 us (1.016); the launches traced: 56.1 us -> 57.8 us
  Pallas kernels: 51.6 us -> 53.2 us
    pallas_call x1, Pallas kernels: 51.6 us -> 53.2 us  [on_device(): pl.pallas_call(functools.partial(kernel, n_rows, n_cols, steps), out_shap...]
where the time goes in v10:
time: 57.9 us; the launch traced here: 57.8 us
  Pallas kernels  53.2 us (92%)
  other arithmetic  2.6 us (4%)
  local copies, waits for them, and re-layouts  1.32 us (2%)
  between operations  0.64 us (1%)
    pallas_call x1, Pallas kernels, on_device(): pl.pallas_call(functools.partial(kernel, n_rows, n_cols, steps), out_shap...  53.2 us
    convert_element_type x1, other arithmetic, on_device(): return (low.astype(jnp.float32), remainder.reshape(rhs.shape))  2.6 us
    unnamed x1, local copies, waits for them, and re-layouts  1.32 us

profile of v10, /device:TPU:2, one launch (start us, length us, event | category | flops | bytes accessed | tf_op | source)
XLA Modules:
  0.0 57.8 jit_solution(11346262798232871939)
XLA Ops:
  0.6 53.2 %shard_map.50 = (bf16[4,512,512]{2,1,0:T(8,128)(2,1)S(1)}, f32[2,512,512]{2,1,0:T(8,128)S(1)}) custom-call(bf16[2,512,512]{2,1,0:T(8,128)(2,1)} %bitcast.7, f32[2,512,512]{2,1,0:T(8,128)} %bitcast.6, bf16[4,512,512]{2,1,0:T(8,128)(2,1)} %inverse.1), custom_call_target="tpu_custom_call" | custom-call | tf_op jit(solution)/shard_map/pallas_call | solution.py:436
  53.9 2.6 %convert_element_type.3 = f32[4,512,512]{2,1,0:T(8,128)} convert(bf16[4,512,512]{2,1,0:T(8,128)(2,1)S(1)} %get-tuple-element.4) | non-fusion elementwise | flops 1048576 | bytes 6291456 | tf_op jit(solution)/shard_map/convert_element_type | solution.py:467
  56.5 1.3 %copy.7 = f32[2,1,512,512]{3,2,1,0:T(8,128)} copy(f32[2,1,512,512]{3,2,1,0:T(8,128)S(1)} %bitcast.5) | data formatting | bytes 4194304

commit v11 on v8

--- a/solution.py
+++ b/solution.py
@@ -212,9 +212,15 @@
             store_low(0, t).start()
             store_rem(0, t).start()
 
-    @pl.when(mine > col)
+    @pl.when((mine > col) & (mine != 1))
     def _():
         send_own(0)
+
+    @pl.when((mine > col) & (mine == 1))
+    def _():
+        load_own(0).wait()
+        for b in range(len(bits)):
+            send_block(0, col, b).start()
 
     @pl.when(mine <= col)
     def _():

time: 57 us -> 57 us (level)
  no operation moved by 1% of the time
where the time goes in v11:
time: 57 us; the launch traced here: 56.1 us
  Pallas kernels  51.6 us (91%)
  other arithmetic  2.6 us (5%)
  local copies, waits for them, and re-layouts  1.32 us (2%)
  between operations  0.64 us (1%)
    pallas_call x1, Pallas kernels, on_device(): pl.pallas_call(functools.partial(kernel, n_rows, n_cols, steps), out_shap...  51.6 us
    convert_element_type x1, other arithmetic, on_device(): return (low.astype(jnp.float32), remainder.reshape(rhs.shape))  2.6 us
    unnamed x1, local copies, waits for them, and re-layouts  1.32 us

profile of v11, /device:TPU:2, one launch (start us, length us, event | category | flops | bytes accessed | tf_op | source)
XLA Modules:
  0.0 56.1 jit_solution(14342093373250055676)
XLA Ops:
  0.6 51.6 %shard_map.50 = (bf16[4,512,512]{2,1,0:T(8,128)(2,1)S(1)}, f32[2,512,512]{2,1,0:T(8,128)S(1)}) custom-call(bf16[2,512,512]{2,1,0:T(8,128)(2,1)} %bitcast.7, f32[2,512,512]{2,1,0:T(8,128)} %bitcast.6, bf16[4,512,512]{2,1,0:T(8,128)(2,1)} %inverse.1), custom_call_target="tpu_custom_call" | custom-call | tf_op jit(solution)/shard_map/pallas_call | solution.py:428
  52.2 2.6 %convert_element_type.3 = f32[4,512,512]{2,1,0:T(8,128)} convert(bf16[4,512,512]{2,1,0:T(8,128)(2,1)S(1)} %get-tuple-element.4) | non-fusion elementwise | flops 1048576 | bytes 6291456 | tf_op jit(solution)/shard_map/convert_element_type | solution.py:459
  54.8 1.3 %copy.7 = f32[2,1,512,512]{3,2,1,0:T(8,128)} copy(f32[2,1,512,512]{3,2,1,0:T(8,128)S(1)} %bitcast.5) | data formatting | bytes 4194304
